TPU v7x, 256 devices: a whole 4x4x8 slice. The times are simulated.
256 devices in a mesh: var: 64 (over x_lo, z, y), samp: 4 (over x_hi, core).
Axes of the slice: x: 4 (x_hi: 2, x_lo: 2; x = x_hi * 2 + x_lo), y: 4, z: 8, core: 2. Of those that a mesh axis runs over, the one named last changes fastest.
Arguments:
- dosages: bfloat16 [8192, 49152], P('samp', 'var'), may hold values from 0 to 2
- observed: int32 [8192, 49152], P('samp', 'var'), may hold values 0 or 1
Outputs:
- ld_scores: float32 [49152], P(('var', 'samp'))
All inputs are finite; a program needn't handle non-finite values. No bound on the sum of `observed` on one device may be relied on, other than what follows from the above.
Results may differ from a plain program's by a relative error of at most 0.00055.
Values may be sent and summed in bfloat16 or wider, within the bound.
A program may use at most 192 MiB of HBM per device.

v0:
```python
import jax
import jax.numpy as jnp
from jax import lax
from jax.sharding import PartitionSpec as P

BAND = 3


def from_behind(value, axis, steps):
    count = lax.axis_size(axis)
    leading, last = (max(0, -steps), min(count, count - steps))
    return lax.ppermute(value, axis, [(source, source + steps) for source in range(leading, last)])


def adjusted_r2(gram_part, samples):
    correl = gram_part / samples
    squared = correl * correl
    return squared - (1.0 - squared) / (samples - 2)


def local(dosages, observed):
    values = dosages.astype(jnp.float32)
    present = observed.astype(jnp.float32)
    seen_count, first_sum, second_sum = lax.psum(
        (jnp.sum(present, 0), jnp.sum(present * values, 0), jnp.sum(present * values * values, 0)),
        "samp",
    )
    seen_count = jnp.maximum(seen_count, 1.0)
    column_mean = first_sum / seen_count
    spread = second_sum / seen_count - column_mean * column_mean
    standard = ((values - column_mean) * lax.rsqrt(spread + 1e-05) * present).astype(jnp.bfloat16)
    samples = standard.shape[0] * lax.axis_size("samp")
    block_width = standard.shape[1]
    position = lax.axis_index("var")
    chain_len = lax.axis_size("var")
    rows_here = block_width // lax.axis_size("samp")
    partners = [standard]
    for offset in range(1, BAND + 1):
        partners.append(from_behind(standard, "var", -offset))
    band_cat = jnp.concatenate(partners, 1)
    gram_part = lax.psum_scatter(
        lax.dot_general(
            standard, band_cat, (((0,), (0,)), ((), ())), preferred_element_type=jnp.float32
        ).astype(jnp.bfloat16),
        "samp",
        scatter_dimension=0,
        tiled=True,
    ).astype(jnp.float32)
    adjusted = adjusted_r2(gram_part, samples).reshape(rows_here, BAND + 1, block_width)
    in_range = (position + jnp.arange(BAND + 1, dtype=jnp.int32) < chain_len).astype(jnp.float32)
    adjusted = adjusted * in_range[None, :, None]
    ld_total = jnp.sum(adjusted, (1, 2))
    col_sums = jnp.sum(adjusted[:, 1:, :], 0)
    shares = lax.psum_scatter(col_sums, "samp", scatter_dimension=1, tiled=True)
    for offset in range(1, BAND + 1):
        ld_total = ld_total + from_behind(shares[offset - 1], "var", offset)
    return ld_total / block_width


def solution(mesh):
    placed = (P("samp", "var"), P("samp", "var"))
    return jax.shard_map(
        local, mesh=mesh, in_specs=placed, out_specs=P(("var", "samp")), check_vma=False
    )
```

profile of v0, /device:TPU:1, one launch (start us, length us, event | category | flops | bytes accessed | tf_op | source)
XLA Modules:
  0.0 504.5 jit_solution(1905817803283281327)
XLA Ops:
  6.5 5.4 %fusion.12 = (f32[768]{0:T(1024)S(1)}, f32[768]{0:T(1024)S(1)}, f32[768]{0:T(1024)S(1)}) fusion(bf16[2048,768]{1,0:T(8,128)(2,1)} %param.2, s32[2048,768]{1,0:T(8,128)} %param.3), kind=kLoop, calls=%fused_computation.16 | loop fusion | flops 11007744 | bytes 9446400 | tf_op jit(solution)/shard_map/reduce_sum | solution.py:25
  12.0 13.5 %all-reduce = (f32[768]{0:T(1024)S(1)}, f32[768]{0:T(1024)S(1)}, f32[768]{0:T(1024)S(1)}) all-reduce(f32[768]{0:T(1024)S(1)} %get-tuple-element.6, f32[768]{0:T(1024)S(1)} %get-tuple-element.7, f32[768]{0:T(1024)S(1)} %get-tuple-element.5), channel_id=1, replica_groups=mesh['var'=64,'samp'=4] {'samp'}, use_global_device_ids=true, to_apply=%region_5.0 | all-reduce | flops 2304 | bytes 18432 | tf_op jit(solution)/shard_map/psum | solution.py:24
  25.5 3.9 fusion.10
  29.4 1.3 collective-permute-start
  30.7 1.3 collective-permute-start.1
  32.0 1.3 collective-permute-start.2
  33.3 131.3 %collective-permute-done = bf16[2048,768]{1,0:T(8,128)(2,1)S(1)} collective-permute-done((bf16[2048,768]{1,0:T(8,128)(2,1)S(1)}, bf16[2048,768]{1,0:T(8,128)(2,1)S(1)}, u32[]{:S(2)}, u32[]{:S(2)}) %collective-permute-start) | collective-permute-done | bytes 3145760 | tf_op jit(solution)/shard_map/ppermute | solution.py:12
  164.6 3.6 collective-permute-done.1
  168.2 1.7 copy-done.2
  170.0 17.6 %fusion.13 = bf16[768,3072]{1,0:T(8,128)(2,1)} fusion(bf16[2048,768]{1,0:T(8,128)(2,1)} %copy-done.1, bf16[2048,768]{1,0:T(8,128)(2,1)} %collective-permute-done.2, bf16[2048,768]{1,0:T(8,128)(2,1)} %copy-done.2, bf16[2048,768]{1,0:T(8,128)(2,1)S(1)} %collective-permute-done), kind=kOutput, calls=%fused_computation.17 | convolution fusion | flops 9716367360 | bytes 17301504 | tf_op jit(solution)/shard_map/dot_general | solution.py:42
  187.6 0.2 reduce-scatter.7.cloned.1.call-start
  188.0 255.3 %reduce-scatter.5.cloned.1.call-done = bf16[192,3072]{1,0:T(8,128)(2,1)} async-done(((bf16[768,3072]{1,0:T(8,128)(2,1)}), bf16[192,3072]{1,0:T(8,128)(2,1)}) %reduce-scatter.5.cloned.1.call-update) | async-done | bytes 1179664 | tf_op jit(solution)/shard_map/reduce_scatter | solution.py:41
  443.3 2.0 multiply_reduce_fusion
  445.3 2.2 reshape.12
  447.5 2.5 fusion.16
  450.0 0.9 copy.3
  451.0 32.4 %reduce-scatter.7.cloned.1.call-done = f32[192,3]{1,0:T(8,128)} async-done(((f32[768,3]{1,0:T(8,128)}), f32[192,3]{1,0:T(8,128)}) %reduce-scatter.7.cloned.1.call-update) | async-done | bytes 2320
  483.4 1.1 fusion.18
  484.6 0.1 copy.5
  484.7 3.1 collective-permute-start.3
  487.9 4.4 collective-permute-start.4
  492.3 4.1 collective-permute-start.5
  496.4 0.7 collective-permute-done.5
  497.1 0.6 add_multiply_fusion
  (18 shorter events, 0.4 us)
Async XLA Ops:
  6.5 18.9 %copy-start = (bf16[2048,768]{1,0:T(8,128)(2,1)S(1)}, bf16[2048,768]{1,0:T(8,128)(2,1)}, u32[]{:S(2)}) copy-start(bf16[2048,768]{1,0:T(8,128)(2,1)} %param.2) | copy-start | bytes 9437188
  6.5 436.8 %reduce-scatter.5.cloned.1.call-start = ((), (), s32[]{:S(2)}) async-start(), calls=%async_computation.2 | async-start | bytes 5898240 | tf_op jit(solution)/shard_map/reduce_scatter | solution.py:41
  29.4 2.6 copy-start.1
  29.4 135.2 %collective-permute-start = (bf16[2048,768]{1,0:T(8,128)(2,1)S(1)}, bf16[2048,768]{1,0:T(8,128)(2,1)S(1)}, u32[]{:S(2)}, u32[]{:S(2)}) collective-permute-start(bf16[2048,768]{1,0:T(8,128)(2,1)S(1)} %fusion.10), channel_id=1, source_target_pairs={{4,0},{8,4},{12,8},{16,12},{20,16},{24,20},{28,24},{32,28},{36,32}... | collective-permute-start | bytes 9437192 | tf_op jit(solution)/shard_map/ppermute | solution.py:12
  30.7 137.5 %collective-permute-start.1 = (bf16[2048,768]{1,0:T(8,128)(2,1)S(1)}, bf16[2048,768]{1,0:T(8,128)(2,1)S(1)}, u32[]{:S(2)}, u32[]{:S(2)}) collective-permute-start(bf16[2048,768]{1,0:T(8,128)(2,1)S(1)} %fusion.10), channel_id=1, source_target_pairs={{8,0},{12,4},{16,8},{20,12},{24,16},{28,20},{32,24},{36,28},{40,32... | collective-permute-start | bytes 9437192 | tf_op jit(solution)/shard_map/ppermute | solution.py:12
  32.0 138.0 %collective-permute-start.2 = (bf16[2048,768]{1,0:T(8,128)(2,1)S(1)}, bf16[2048,768]{1,0:T(8,128)(2,1)}, u32[]{:S(2)}, u32[]{:S(2)}) collective-permute-start(bf16[2048,768]{1,0:T(8,128)(2,1)S(1)} %fusion.10), channel_id=1, source_target_pairs={{12,0},{16,4},{20,8},{24,12},{28,16},{32,20},{36,24},{40,28},{44,3... | collective-permute-start | bytes 9437192 | tf_op jit(solution)/shard_map/ppermute | solution.py:12
  168.2 1.8 copy-start.2
  187.6 295.8 %reduce-scatter.7.cloned.1.call-start = ((), (), s32[]{:S(2)}) async-start(), calls=%async_computation.3 | async-start | bytes 491520
  484.7 11.7 %collective-permute-start.3 = (f32[192]{0:T(256)S(1)}, f32[192]{0:T(256)S(1)}, u32[]{:S(2)}, u32[]{:S(2)}) collective-permute-start(f32[192]{0:T(256)S(1)} %bitcast.8), channel_id=1, source_target_pairs={{0,4},{4,8},{8,12},{12,16},{16,20},{20,24},{24,28},{28,32},{32,36}... | collective-permute-start | bytes 2312 | tf_op jit(solution)/shard_map/ppermute | solution.py:12
  487.9 8.5 %collective-permute-start.4 = (f32[192]{0:T(256)S(1)}, f32[192]{0:T(256)S(1)}, u32[]{:S(2)}, u32[]{:S(2)}) collective-permute-start(f32[192]{0:T(256)S(1)} %bitcast.9), channel_id=1, source_target_pairs={{0,8},{4,12},{8,16},{12,20},{16,24},{20,28},{24,32},{28,36},{32,40... | collective-permute-start | bytes 2312 | tf_op jit(solution)/shard_map/ppermute | solution.py:12
  492.3 4.8 collective-permute-start.5
Sparse Core Ops, SparseCore 0:
  187.8 255.5 reduce-scatter.4
  451.1 32.2 reduce-scatter.6
where the time goes:
time: 507 us; the launch traced here: 504 us
  waiting for transfers between devices  423 us (83%)
  matrix products  17.6 us (3%)
  starting transfers between devices  15.6 us (3%)
  other arithmetic  14.4 us (3%)
  blocking collectives  13.5 us (3%)
  between operations  13.5 us (3%)
  local copies, waits for them, and re-layouts  6.46 us (1%)
    reduce_scatter x1, waiting for transfers between devices, local(): lax.psum_scatter(lax.dot_general(standard, band_cat, (((0,), (0,)), ((),...  255 us
    ppermute x6, waiting for transfers between devices, from_behind(): lax.ppermute(value, axis, [(source, source + steps) for source in range(l...  136 us
    unnamed x3, waiting for transfers between devices  32.5 us
    dot_general x1, matrix products, local(): lax.dot_general(standard, band_cat, (((0,), (0,)), ((), ())), preferred_e...  17.6 us
    ppermute x6, starting transfers between devices, from_behind(): lax.ppermute(value, axis, [(source, source + steps) for source in range(l...  15.4 us
    psum x1, blocking collectives, local(): lax.psum((jnp.sum(present, 0), jnp.sum(present * values, 0), jnp.sum(pres...  13.5 us
  transfers between devices with their start and end apart: 8, of which 5 were waited for; matrix products, arithmetic and copies ran while one was open for 0% of the time, Pallas kernels for 0%

commit v1 on v0

v1 whole, which is shorter than its diff:
```python
import functools

import jax
import jax.numpy as jnp
from jax import lax
from jax.experimental import pallas as pl
from jax.experimental.pallas import tpu as pltpu
from jax.sharding import PartitionSpec as P

MESH = pl.DeviceIdType.MESH
BAND = 3
LANES = 128
RING = 4
PIECES = 2
F32 = jnp.float32
BF16 = jnp.bfloat16


def plan(chunks):
    width = chunks * LANES
    units = [("own", k, width, 2 * LANES) for k in range(chunks // 2)]
    for j in range(chunks):
        units.append(("both", j, width, 2 * LANES))
        units.append(("down", j, LANES * (j + 1), LANES))
        if j:
            units.append(("across", j, LANES, LANES * j))
    return units


def kernel(chain, units, dose_hbm, seen_hbm, out_ref, dose, seen, own, near, far, relay, stat, stat_in,
           row_own, row_near, col_near, col_far, share, share_in, *rest):
    count = len(units)
    part, half_out, half_in, quarter_out, quarter_in = [rest[i * count:(i + 1) * count] for i in range(5)]
    (load_sem, stat_send, stat_recv, near_send, near_recv, far_send, far_recv, hop_send, hop_recv, relay_send,
     half_send, half_recv, quarter_send, quarter_recv, share_send, share_recv) = rest[5 * count:]
    depth, width = dose.shape
    chunks = width // LANES
    quarter = width // 4
    samples = 4 * depth
    v = lax.axis_index("var")
    s = lax.axis_index("samp")
    core = lax.rem(s, 2)
    side = s // 2
    y = lax.rem(v, RING)
    first_in_ring = y == 0
    last_in_ring = y == RING - 1

    def at(step, member=None):
        return (lax.rem(v + step + chain, chain), s if member is None else member)

    mate = (v, s + 1 - 2 * core)
    opposite = (v, lax.rem(s + 2, 4))

    def cols(j):
        return pl.ds(j * LANES, LANES)

    loads = []
    for j in range(chunks):
        loads.append((
            pltpu.make_async_copy(dose_hbm.at[:, cols(j)], dose.at[:, cols(j)], load_sem.at[0, j]),
            pltpu.make_async_copy(seen_hbm.at[:, cols(j)], seen.at[:, cols(j)], load_sem.at[1, j])))
        for copy in loads[-1]:
            copy.start()

    barrier = pltpu.get_barrier_semaphore()
    friends = [(v, lax.rem(s + k, 4)) for k in (1, 2, 3)]
    for step in (1, 3):
        friends += [at(step, q) for q in range(4)] + [at(-step, q) for q in range(4)]
    friends += [at(4), at(-4)]
    for friend in friends:
        pl.semaphore_signal(barrier, inc=1, device_id=friend, device_id_type=MESH)

    row_own[...] = jnp.zeros_like(row_own)
    row_near[...] = jnp.zeros_like(row_near)
    col_near[...] = jnp.zeros_like(col_near)
    col_far[...] = jnp.zeros_like(col_far)

    block = min(256, depth)

    def sum_chunk(j):
        def body(r, acc):
            rows = pl.ds(pl.multiple_of(r * block, block), block)
            present = seen[rows, cols(j)].astype(F32)
            values = dose[rows, cols(j)].astype(F32)
            weighted = present * values
            terms = (present, weighted, weighted * values)
            return tuple(a + jnp.sum(t.reshape(block // 8, 8, LANES), 0) for a, t in zip(acc, terms))

        zero = jnp.zeros((8, LANES), F32)
        sums = lax.fori_loop(0, depth // block, body, (zero, zero, zero))
        for i, total in enumerate(sums):
            stat[j, i:i + 1, :] = jnp.sum(total, 0, keepdims=True)

    def stat_copy(j, k):
        return pltpu.make_async_remote_copy(
            src_ref=stat.at[j], dst_ref=stat_in.at[k - 1, j], send_sem=stat_send.at[k - 1, j],
            recv_sem=stat_recv.at[k - 1, j], device_id=(v, lax.rem(s + k, 4)), device_id_type=MESH)

    def piece(ref, j, p):
        rows = depth // PIECES
        return ref.at[pl.ds(p * rows, rows), cols(j)]

    def near_copy(j):
        return pltpu.make_async_remote_copy(
            src_ref=own.at[:, cols(j)], dst_ref=near.at[:, cols(j)], send_sem=near_send.at[j],
            recv_sem=near_recv.at[j], device_id=at(-1), device_id_type=MESH)

    def hop_copy(j, p):
        return pltpu.make_async_remote_copy(
            src_ref=piece(own, j, p), dst_ref=piece(relay, j, p), send_sem=hop_send.at[j, p],
            recv_sem=hop_recv.at[j, p], device_id=at(3), device_id_type=MESH)

    def relay_copy(j, p):
        return pltpu.make_async_remote_copy(
            src_ref=piece(relay, j, p), dst_ref=piece(near, j, p), send_sem=relay_send.at[j, p],
            recv_sem=near_recv.at[j], device_id=at(-4), device_id_type=MESH)

    def far_copy(j):
        return pltpu.make_async_remote_copy(
            src_ref=own.at[:, cols(j)], dst_ref=far.at[:, cols(j)], send_sem=far_send.at[j],
            recv_sem=far_recv.at[j], device_id=at(-3), device_id_type=MESH)

    def standardize(j):
        for k in (1, 2, 3):
            stat_copy(j, k).wait_recv()
        sums = stat[j] + stat_in[0, j] + stat_in[1, j] + stat_in[2, j]
        seen_count = jnp.maximum(sums[0:1], 1.0)
        mean = sums[1:2] / seen_count
        spread = sums[2:3] / seen_count - mean * mean
        scale = lax.rsqrt(spread + 1e-05)

        def body(r, carry):
            rows = pl.ds(pl.multiple_of(r * block, block), block)
            present = seen[rows, cols(j)].astype(F32)
            values = dose[rows, cols(j)].astype(F32)
            own[rows, cols(j)] = ((values - mean) * scale * present).astype(BF16)
            return carry

        lax.fori_loop(0, depth // block, body, 0)
        far_copy(j).start()

        @pl.when(first_in_ring)
        def _():
            for p in range(PIECES):
                hop_copy(j, p).start()

        @pl.when(jnp.logical_not(first_in_ring))
        def _():
            near_copy(j).start()

    for j in range(chunks + 2):
        if j < chunks:
            for copy in loads[j]:
                copy.wait()
            stat[j] = jnp.zeros((8, LANES), F32)
            sum_chunk(j)
            if j == 0:
                pl.semaphore_wait(barrier, len(friends))
            for k in (1, 2, 3):
                stat_copy(j, k).start()
        if j >= 2:
            standardize(j - 2)

    keep_near = jnp.where(v + 1 < chain, 1.0, 0.0).astype(F32)
    keep_far = jnp.where(v + 3 < chain, 1.0, 0.0).astype(F32)
    keep_cross = jnp.where(lax.rem(v + 1, chain) + 2 < chain, 1.0, 0.0).astype(F32)

    def dot(a, b):
        return lax.dot_general(a, b, (((0,), (0,)), ((), ())), preferred_element_type=F32)

    def half_copy(u):
        return pltpu.make_async_remote_copy(
            src_ref=half_out[u], dst_ref=half_in[u], send_sem=half_send.at[u], recv_sem=half_recv.at[u],
            device_id=mate, device_id_type=MESH)

    def quarter_copy(u):
        return pltpu.make_async_remote_copy(
            src_ref=quarter_out[u], dst_ref=quarter_in[u], send_sem=quarter_send.at[u],
            recv_sem=quarter_recv.at[u], device_id=opposite, device_id_type=MESH)

    def rows_of(u, index):
        size = units[u][2] // 4
        return pl.ds(pl.multiple_of(index * size, size), size)

    def multiply(u):
        kind, j, _, _ = units[u]
        if kind == "own":
            part[u][...] = dot(own[...], own[:, 2 * j * LANES:2 * (j + 1) * LANES])
        elif kind == "both":
            part[u][...] = dot(own[...], jnp.concatenate([near[:, cols(j)], far[:, cols(j)]], 1))
        elif kind == "down":
            part[u][...] = dot(near[:, :LANES * (j + 1)], far[:, cols(j)])
        else:
            part[u][...] = dot(near[:, cols(j)], far[:, :LANES * j])
        for p in range(2):
            half_out[u][p] = part[u][rows_of(u, 2 * p + 1 - core), :].astype(BF16)
        half_copy(u).start()

    def fold_mate(u):
        half_copy(u).wait_recv()
        away = rows_of(u, 2 * (1 - side) + core)
        quarter_out[u][...] = (part[u][away, :] + half_in[u][1 - side].astype(F32)).astype(BF16)
        quarter_copy(u).start()
        home = rows_of(u, s)
        part[u][home, :] = part[u][home, :] + half_in[u][side].astype(F32)

    def by_lane(x):
        total = x[:, :LANES]
        for i in range(1, x.shape[1] // LANES):
            total = total + x[:, i * LANES:(i + 1) * LANES]
        return total

    def by_sublane(x):
        return jnp.sum(x.reshape(x.shape[0] // 8, 8, x.shape[1]), 0)

    def fold_opposite(u):
        quarter_copy(u).wait_recv()
        kind, j, rows, columns = units[u]
        total = part[u][rows_of(u, s), :] + quarter_in[u][...].astype(F32)
        square = total * total
        if kind == "own":
            row_own[:quarter, :] += by_lane(square)
        elif kind == "both":
            to_near = square[:, :LANES] * keep_near
            to_far = square[:, LANES:] * keep_far
            row_own[:quarter, :] += to_near + to_far
            col_near[:, cols(j)] += by_sublane(to_near)
            col_far[:, cols(j)] += by_sublane(to_far)
        else:
            square = square * keep_cross
            size = rows // 4
            start = s * size if kind == "down" else LANES * j + s * size
            where = pl.ds(pl.multiple_of(start, size), size)
            row_near[where, :] += by_lane(square)
            if kind == "down":
                col_far[:, cols(j)] += by_sublane(square)
            else:
                col_far[:, :columns] += by_sublane(square)

    def arrive(j):
        @pl.when(last_in_ring)
        def _():
            for p in range(PIECES):
                hop_copy(j, p).wait_recv()
                relay_copy(j, p).start()

        far_copy(j).wait_recv()
        near_copy(j).wait_recv()

    for u in range(count + 2):
        if u < count:
            if units[u][0] == "both":
                arrive(units[u][1])
            multiply(u)
        if 1 <= u <= count:
            fold_mate(u - 1)
        if u >= 2:
            fold_opposite(u - 2)

    near_sum = jnp.sum(row_near[...].T, 0, keepdims=True) + jnp.sum(col_near[...], 0, keepdims=True)
    far_sum = jnp.sum(col_far[...], 0, keepdims=True)

    def share_copy(i, q):
        return pltpu.make_async_remote_copy(
            src_ref=share.at[i, q], dst_ref=share_in.at[i, s], send_sem=share_send.at[i, q],
            recv_sem=share_recv.at[i, s], device_id=at((1, 3)[i], q), device_id_type=MESH)

    def share_arrival(i, q):
        return pltpu.make_async_remote_copy(
            src_ref=share.at[i, q], dst_ref=share_in.at[i, q], send_sem=share_send.at[i, q],
            recv_sem=share_recv.at[i, q], device_id=at((1, 3)[i], q), device_id_type=MESH)

    for i, total in enumerate((near_sum, far_sum)):
        wide = jnp.broadcast_to(total, (8, width))
        for q in range(4):
            turned = wide if q == 0 else pltpu.roll(wide, width - q * quarter, 1)
            share[i, q] = turned[:, :2 * LANES]
            share_copy(i, q).start()
    row_total = jnp.sum(row_own[...].T, 0, keepdims=True)
    for i in range(2):
        for q in range(4):
            share_arrival(i, q).wait_recv()
            row_total = row_total + share_in[i, q, 0:1, :]
    pairs = (1 + jnp.minimum(v, BAND) + jnp.minimum(chain - 1 - v, BAND)).astype(F32)
    squares = row_total * (1.0 / (samples * samples))
    result = squares / width + (squares / width - pairs) / (samples - 2)
    out_ref[...] = result[:, :quarter]

    for j in range(chunks):
        for k in (1, 2, 3):
            stat_copy(j, k).wait_send()
        far_copy(j).wait_send()

    @pl.when(first_in_ring)
    def _():
        for j in range(chunks):
            for p in range(PIECES):
                hop_copy(j, p).wait_send()

    @pl.when(jnp.logical_not(first_in_ring))
    def _():
        for j in range(chunks):
            near_copy(j).wait_send()

    @pl.when(last_in_ring)
    def _():
        for j in range(chunks):
            for p in range(PIECES):
                relay_copy(j, p).wait_send()

    for u in range(count):
        half_copy(u).wait_send()
        quarter_copy(u).wait_send()
    for i in range(2):
        for q in range(4):
            share_copy(i, q).wait_send()


def local(chain, dosages, observed):
    depth, width = dosages.shape
    chunks = width // LANES
    units = plan(chunks)
    count = len(units)
    dma = pltpu.SemaphoreType.DMA
    scratch = [
        pltpu.VMEM((depth, width), BF16),
        pltpu.VMEM((depth, width), jnp.int32),
        pltpu.VMEM((depth, width), BF16),
        pltpu.VMEM((depth, width), BF16),
        pltpu.VMEM((depth, width), BF16),
        pltpu.VMEM((depth, width), BF16),
        pltpu.VMEM((chunks, 8, LANES), F32),
        pltpu.VMEM((3, chunks, 8, LANES), F32),
        pltpu.VMEM((2 * LANES, LANES), F32),
        pltpu.VMEM((width, LANES), F32),
        pltpu.VMEM((8, width), F32),
        pltpu.VMEM((8, width), F32),
        pltpu.VMEM((2, 4, 8, 2 * LANES), F32),
        pltpu.VMEM((2, 4, 8, 2 * LANES), F32),
    ]
    scratch += [pltpu.VMEM((rows, columns), F32) for _, _, rows, columns in units]
    for _ in range(2):
        scratch += [pltpu.VMEM((2, rows // 4, columns), BF16) for _, _, rows, columns in units]
    for _ in range(2):
        scratch += [pltpu.VMEM((rows // 4, columns), BF16) for _, _, rows, columns in units]
    scratch += [
        dma((2, chunks)), dma((3, chunks)), dma((3, chunks)),
        dma((chunks,)), dma((chunks,)), dma((chunks,)), dma((chunks,)),
        dma((chunks, PIECES)), dma((chunks, PIECES)), dma((chunks, PIECES)),
        dma((count,)), dma((count,)), dma((count,)), dma((count,)),
        dma((2, 4)), dma((2, 4)),
    ]
    out = pl.pallas_call(
        functools.partial(kernel, chain, units),
        out_shape=jax.ShapeDtypeStruct((1, width // 4), F32),
        in_specs=[pl.BlockSpec(memory_space=pl.ANY)] * 2,
        out_specs=pl.BlockSpec(memory_space=pltpu.VMEM),
        scratch_shapes=scratch,
        compiler_params=pltpu.CompilerParams(
            collective_id=0, has_side_effects=True, vmem_limit_bytes=56 * 2**20),
    )(dosages, observed)
    return out.reshape(width // 4)


def solution(mesh):
    placed = (P("samp", "var"), P("samp", "var"))
    return jax.shard_map(
        functools.partial(local, mesh.shape["var"]), mesh=mesh, in_specs=placed,
        out_specs=P(("var", "samp")), check_vma=False)
```

time: 507 us -> 170 us (0.34)
  the two profiles are of different devices: /device:TPU:1 before, /device:TPU:97 now
where the time goes in v1:
time: 170 us
  Pallas kernels  169 us (99%)
    pallas_call x1, Pallas kernels, local(): pl.pallas_call(functools.partial(kernel, chain, units), out_shape=jax.Sha...  169 us

profile of v1, /device:TPU:97, one launch (start us, length us, event | category | flops | bytes accessed | tf_op | source)
XLA Modules:
  0.0 170.0 jit_solution(16822143898490373697)
XLA Ops:
  0.0 168.8 %shard_map.28 = f32[1,192]{1,0:T(1,128)} custom-call(bf16[2048,768]{1,0:T(8,128)(2,1)} %dose_hbm.1, s32[2048,768]{1,0:T(8,128)} %seen_hbm.1), custom_call_target="tpu_custom_call" | custom-call | tf_op jit(solution)/shard_map/pallas_call | solution.py:353
  168.8 1.2 copy.4

commit v2 on v1

--- a/solution.py
+++ b/solution.py
@@ -11,7 +11,7 @@
 BAND = 3
 LANES = 128
 RING = 4
-PIECES = 2
+PIECES = 4
 F32 = jnp.float32
 BF16 = jnp.bfloat16
 
@@ -31,7 +31,7 @@
            row_own, row_near, col_near, col_far, share, share_in, *rest):
     count = len(units)
     part, half_out, half_in, quarter_out, quarter_in = [rest[i * count:(i + 1) * count] for i in range(5)]
-    (load_sem, stat_send, stat_recv, near_send, near_recv, far_send, far_recv, hop_send, hop_recv, relay_send,
+    (load_sem, stat_send, stat_recv, near_send, near_recv, far_send, far_recv, edge_send, hop_send, hop_recv, relay_send,
      half_send, half_recv, quarter_send, quarter_recv, share_send, share_recv) = rest[5 * count:]
     depth, width = dose.shape
     chunks = width // LANES
@@ -42,6 +42,9 @@
     core = lax.rem(s, 2)
     side = s // 2
     y = lax.rem(v, RING)
+    edge = lax.rem(v, chain // 2) < RING
+    leaves = jnp.logical_and(edge, y != RING - 1)
+    lands = jnp.logical_and(lax.rem(v, chain // 2) >= chain // 2 - RING, y != RING - 1)
     first_in_ring = y == 0
     last_in_ring = y == RING - 1
 
@@ -67,6 +70,9 @@
     for step in (1, 3):
         friends += [at(step, q) for q in range(4)] + [at(-step, q) for q in range(4)]
     friends += [at(4), at(-4)]
+    across = chain // 2
+    if across > 4:
+        friends += [at(step) for step in (across + 3, -across - 3, across - 4, 4 - across, across + 1, -across - 1)]
     for friend in friends:
         pl.semaphore_signal(barrier, inc=1, device_id=friend, device_id_type=MESH)
 
@@ -108,17 +114,53 @@
     def hop_copy(j, p):
         return pltpu.make_async_remote_copy(
             src_ref=piece(own, j, p), dst_ref=piece(relay, j, p), send_sem=hop_send.at[j, p],
-            recv_sem=hop_recv.at[j, p], device_id=at(3), device_id_type=MESH)
-
-    def relay_copy(j, p):
-        return pltpu.make_async_remote_copy(
-            src_ref=piece(relay, j, p), dst_ref=piece(near, j, p), send_sem=relay_send.at[j, p],
-            recv_sem=near_recv.at[j], device_id=at(-4), device_id_type=MESH)
+            recv_sem=hop_recv.at[j, p], device_id=at(jnp.where(edge, across + 3, 3) if p < 1 else 3), device_id_type=MESH)
+
+    def relay_copy(j, p, target, sem, step):
+        return pltpu.make_async_remote_copy(
+            src_ref=piece(relay, j, p), dst_ref=piece(target, j, p), send_sem=relay_send.at[j, p],
+            recv_sem=sem.at[j], device_id=at(step), device_id_type=MESH)
+
+    def near_relay(j, p):
+        return relay_copy(j, p, near, near_recv, jnp.where(edge, across - 4, -4) if p < 1 else -4)
+
+    def far_relay(j, p):
+        return relay_copy(j, p, far, far_recv, across + 1)
 
     def far_copy(j):
         return pltpu.make_async_remote_copy(
             src_ref=own.at[:, cols(j)], dst_ref=far.at[:, cols(j)], send_sem=far_send.at[j],
             recv_sem=far_recv.at[j], device_id=at(-3), device_id_type=MESH)
+
+    def direct_copy(j, p):
+        return pltpu.make_async_remote_copy(
+            src_ref=piece(own, j, p), dst_ref=piece(far, j, p), send_sem=edge_send.at[j, p],
+            recv_sem=far_recv.at[j], device_id=at(-3), device_id_type=MESH)
+
+    def cross_copy(j, p):
+        return pltpu.make_async_remote_copy(
+            src_ref=piece(own, j, p), dst_ref=piece(relay, j, p), send_sem=edge_send.at[j, p],
+            recv_sem=hop_recv.at[j, p], device_id=at(across - 4), device_id_type=MESH)
+
+    def each_send(j, act):
+        @pl.when(jnp.logical_not(leaves))
+        def _():
+            act(far_copy(j))
+
+        @pl.when(leaves)
+        def _():
+            for p in range(2):
+                act(cross_copy(j, p))
+                act(direct_copy(j, p + 2))
+
+        @pl.when(first_in_ring)
+        def _():
+            for p in range(PIECES):
+                act(hop_copy(j, p))
+
+        @pl.when(jnp.logical_not(first_in_ring))
+        def _():
+            act(near_copy(j))
 
     def standardize(j):
         for k in (1, 2, 3):
@@ -137,16 +179,28 @@
             return carry
 
         lax.fori_loop(0, depth // block, body, 0)
-        far_copy(j).start()
-
-        @pl.when(first_in_ring)
-        def _():
-            for p in range(PIECES):
-                hop_copy(j, p).start()
-
-        @pl.when(jnp.logical_not(first_in_ring))
-        def _():
-            near_copy(j).start()
+
+        each_send(j, lambda copy: copy.start())
+
+    hops = [(j, p) for j in range(chunks) for p in range(PIECES)]
+    passed = []
+
+    def pass_on(until):
+        ready = [hop for hop in hops if hop < until and hop not in passed]
+        passed.extend(ready)
+
+        @pl.when(last_in_ring)
+        def _():
+            for j, p in ready:
+                hop_copy(j, p).wait_recv()
+                near_relay(j, p).start()
+
+        @pl.when(lands)
+        def _():
+            for j, p in ready:
+                if p < 2:
+                    hop_copy(j, p).wait_recv()
+                    far_relay(j, p).start()
 
     for j in range(chunks + 2):
         if j < chunks:
@@ -160,6 +214,8 @@
                 stat_copy(j, k).start()
         if j >= 2:
             standardize(j - 2)
+        if j >= chunks:
+            pass_on((0, j - chunks + 1))
 
     keep_near = jnp.where(v + 1 < chain, 1.0, 0.0).astype(F32)
     keep_far = jnp.where(v + 3 < chain, 1.0, 0.0).astype(F32)
@@ -237,25 +293,34 @@
             else:
                 col_far[:, :columns] += by_sublane(square)
 
-    def arrive(j):
-        @pl.when(last_in_ring)
-        def _():
-            for p in range(PIECES):
-                hop_copy(j, p).wait_recv()
-                relay_copy(j, p).start()
-
-        far_copy(j).wait_recv()
-        near_copy(j).wait_recv()
-
-    for u in range(count + 2):
-        if u < count:
-            if units[u][0] == "both":
-                arrive(units[u][1])
+    groups = [[u for u in range(count) if units[u][0] == "own"]]
+    for j in range(chunks):
+        groups.append([u for u in range(count) if units[u][0] != "own" and units[u][1] == j])
+    to_mate, to_opposite = [], []
+
+    def drain(group):
+        while to_opposite and to_opposite[0][0] <= group:
+            fold_opposite(to_opposite.pop(0)[1])
+
+    for g, group in enumerate(groups):
+        if g:
+            pass_on((g, PIECES - 1))
+            far_copy(g - 1).wait_recv()
+            near_copy(g - 1).wait_recv()
+        for i, u in enumerate(group):
             multiply(u)
-        if 1 <= u <= count:
-            fold_mate(u - 1)
-        if u >= 2:
-            fold_opposite(u - 2)
+            if to_mate:
+                done = to_mate.pop(0)
+                fold_mate(done[1])
+                to_opposite.append(done)
+            to_mate.append((g, u))
+            pass_on((g, i + 2))
+            drain(g - 4)
+        pass_on((g, PIECES))
+    for done in to_mate:
+        fold_mate(done[1])
+        to_opposite.append(done)
+    drain(chunks)
 
     near_sum = jnp.sum(row_near[...].T, 0, keepdims=True) + jnp.sum(col_near[...], 0, keepdims=True)
     far_sum = jnp.sum(col_far[...], 0, keepdims=True)
@@ -289,24 +354,18 @@
     for j in range(chunks):
         for k in (1, 2, 3):
             stat_copy(j, k).wait_send()
-        far_copy(j).wait_send()
-
-    @pl.when(first_in_ring)
-    def _():
-        for j in range(chunks):
-            for p in range(PIECES):
-                hop_copy(j, p).wait_send()
-
-    @pl.when(jnp.logical_not(first_in_ring))
-    def _():
-        for j in range(chunks):
-            near_copy(j).wait_send()
+        each_send(j, lambda copy: copy.wait_send())
 
     @pl.when(last_in_ring)
     def _():
-        for j in range(chunks):
-            for p in range(PIECES):
-                relay_copy(j, p).wait_send()
+        for j, p in hops:
+            near_relay(j, p).wait_send()
+
+    @pl.when(lands)
+    def _():
+        for j, p in hops:
+            if p < 2:
+                far_relay(j, p).wait_send()
 
     for u in range(count):
         half_copy(u).wait_send()
@@ -346,7 +405,7 @@
     scratch += [
         dma((2, chunks)), dma((3, chunks)), dma((3, chunks)),
         dma((chunks,)), dma((chunks,)), dma((chunks,)), dma((chunks,)),
-        dma((chunks, PIECES)), dma((chunks, PIECES)), dma((chunks, PIECES)),
+        dma((chunks, PIECES)), dma((chunks, PIECES)), dma((chunks, PIECES)), dma((chunks, PIECES)),
         dma((count,)), dma((count,)), dma((count,)), dma((count,)),
         dma((2, 4)), dma((2, 4)),
     ]

time: 170 us -> 126 us (0.74)
  the two profiles are of different devices: /device:TPU:97 before, /device:TPU:1 now
where the time goes in v2:
time: 126 us
  Pallas kernels  125 us (99%)
    pallas_call x1, Pallas kernels, local(): pl.pallas_call(functools.partial(kernel, chain, units), out_shape=jax.Sha...  125 us

profile of v2, /device:TPU:1, one launch (start us, length us, event | category | flops | bytes accessed | tf_op | source)
XLA Modules:
  0.0 126.1 jit_solution(6352966406426903093)
XLA Ops:
  0.0 124.9 %shard_map.28 = f32[1,192]{1,0:T(1,128)} custom-call(bf16[2048,768]{1,0:T(8,128)(2,1)} %dose_hbm.1, s32[2048,768]{1,0:T(8,128)} %seen_hbm.1), custom_call_target="tpu_custom_call" | custom-call | tf_op jit(solution)/shard_map/pallas_call | solution.py:412
  124.9 1.2 copy.4

commit v3 on v2

--- a/solution.py
+++ b/solution.py
@@ -12,6 +12,8 @@
 LANES = 128
 RING = 4
 PIECES = 4
+NEAR_SIDE = 1
+FAR_SIDE = (1, 2)
 F32 = jnp.float32
 BF16 = jnp.bfloat16
 
@@ -44,7 +46,6 @@
     y = lax.rem(v, RING)
     edge = lax.rem(v, chain // 2) < RING
     leaves = jnp.logical_and(edge, y != RING - 1)
-    lands = jnp.logical_and(lax.rem(v, chain // 2) >= chain // 2 - RING, y != RING - 1)
     first_in_ring = y == 0
     last_in_ring = y == RING - 1
 
@@ -72,7 +73,7 @@
     friends += [at(4), at(-4)]
     across = chain // 2
     if across > 4:
-        friends += [at(step) for step in (across + 3, -across - 3, across - 4, 4 - across, across + 1, -across - 1)]
+        friends += [at(step) for step in (across, across + 3, -across - 3, across - 4, 4 - across)]
     for friend in friends:
         pl.semaphore_signal(barrier, inc=1, device_id=friend, device_id_type=MESH)
 
@@ -106,52 +107,69 @@
         rows = depth // PIECES
         return ref.at[pl.ds(p * rows, rows), cols(j)]
 
-    def near_copy(j):
-        return pltpu.make_async_remote_copy(
-            src_ref=own.at[:, cols(j)], dst_ref=near.at[:, cols(j)], send_sem=near_send.at[j],
-            recv_sem=near_recv.at[j], device_id=at(-1), device_id_type=MESH)
+    def halves(j):
+        return (0, 1) if j == chunks - 1 else (0,)
+
+    def span(ref, j, h):
+        rows = depth // len(halves(j))
+        return ref.at[pl.ds(h * rows, rows), cols(j)]
+
+    def slot(j, p):
+        return j + p // (PIECES // len(halves(j)))
+
+    def near_copy(j, h):
+        return pltpu.make_async_remote_copy(
+            src_ref=span(own, j, h), dst_ref=span(near, j, h), send_sem=near_send.at[j + h],
+            recv_sem=near_recv.at[j + h], device_id=at(-1), device_id_type=MESH)
 
     def hop_copy(j, p):
         return pltpu.make_async_remote_copy(
             src_ref=piece(own, j, p), dst_ref=piece(relay, j, p), send_sem=hop_send.at[j, p],
-            recv_sem=hop_recv.at[j, p], device_id=at(jnp.where(edge, across + 3, 3) if p < 1 else 3), device_id_type=MESH)
+            recv_sem=hop_recv.at[j, p], device_id=at(jnp.where(edge, across + 3, 3) if p < NEAR_SIDE else 3), device_id_type=MESH)
 
     def relay_copy(j, p, target, sem, step):
         return pltpu.make_async_remote_copy(
             src_ref=piece(relay, j, p), dst_ref=piece(target, j, p), send_sem=relay_send.at[j, p],
-            recv_sem=sem.at[j], device_id=at(step), device_id_type=MESH)
+            recv_sem=sem.at[slot(j, p)], device_id=at(step), device_id_type=MESH)
 
     def near_relay(j, p):
-        return relay_copy(j, p, near, near_recv, jnp.where(edge, across - 4, -4) if p < 1 else -4)
+        return relay_copy(j, p, near, near_recv, jnp.where(edge, across - 4, -4) if p < NEAR_SIDE else -4)
 
     def far_relay(j, p):
-        return relay_copy(j, p, far, far_recv, across + 1)
-
-    def far_copy(j):
-        return pltpu.make_async_remote_copy(
-            src_ref=own.at[:, cols(j)], dst_ref=far.at[:, cols(j)], send_sem=far_send.at[j],
-            recv_sem=far_recv.at[j], device_id=at(-3), device_id_type=MESH)
+        return relay_copy(j, p, far, far_recv, across - 3)
+
+    def far_copy(j, h):
+        return pltpu.make_async_remote_copy(
+            src_ref=span(own, j, h), dst_ref=span(far, j, h), send_sem=far_send.at[j + h],
+            recv_sem=far_recv.at[j + h], device_id=at(-3), device_id_type=MESH)
 
     def direct_copy(j, p):
         return pltpu.make_async_remote_copy(
             src_ref=piece(own, j, p), dst_ref=piece(far, j, p), send_sem=edge_send.at[j, p],
-            recv_sem=far_recv.at[j], device_id=at(-3), device_id_type=MESH)
+            recv_sem=far_recv.at[slot(j, p)], device_id=at(-3), device_id_type=MESH)
 
     def cross_copy(j, p):
         return pltpu.make_async_remote_copy(
             src_ref=piece(own, j, p), dst_ref=piece(relay, j, p), send_sem=edge_send.at[j, p],
-            recv_sem=hop_recv.at[j, p], device_id=at(across - 4), device_id_type=MESH)
+            recv_sem=hop_recv.at[j, p], device_id=at(across), device_id_type=MESH)
+
+    def by_side(act_side, act_straight):
+        for here, count_side in ((first_in_ring, FAR_SIDE[0]), (jnp.logical_not(first_in_ring), FAR_SIDE[1])):
+            @pl.when(jnp.logical_and(leaves, here))
+            def _(count_side=count_side):
+                for p in range(PIECES):
+                    (act_side if p < count_side else act_straight)(p)
+
+    def each_direct(j, act):
+        by_side(lambda p: None, lambda p: act(direct_copy(j, p)))
 
     def each_send(j, act):
         @pl.when(jnp.logical_not(leaves))
         def _():
-            act(far_copy(j))
-
-        @pl.when(leaves)
-        def _():
-            for p in range(2):
-                act(cross_copy(j, p))
-                act(direct_copy(j, p + 2))
+            for h in halves(j):
+                act(far_copy(j, h))
+
+        by_side(lambda p: act(cross_copy(j, p)), lambda p: None)
 
         @pl.when(first_in_ring)
         def _():
@@ -160,7 +178,8 @@
 
         @pl.when(jnp.logical_not(first_in_ring))
         def _():
-            act(near_copy(j))
+            for h in halves(j):
+                act(near_copy(j, h))
 
     def standardize(j):
         for k in (1, 2, 3):
@@ -181,6 +200,8 @@
         lax.fori_loop(0, depth // block, body, 0)
 
         each_send(j, lambda copy: copy.start())
+        if j < 2:
+            each_direct(j, lambda copy: copy.start())
 
     hops = [(j, p) for j in range(chunks) for p in range(PIECES)]
     passed = []
@@ -195,12 +216,17 @@
                 hop_copy(j, p).wait_recv()
                 near_relay(j, p).start()
 
-        @pl.when(lands)
-        def _():
-            for j, p in ready:
-                if p < 2:
+        for j, q in ready:
+            def hand_on(p):
+                if p == q:
                     hop_copy(j, p).wait_recv()
                     far_relay(j, p).start()
+
+            by_side(hand_on, lambda p: None)
+
+        for j, p in ready:
+            if p == 1 and j + 2 < chunks:
+                each_direct(j + 2, lambda copy: copy.start())
 
     for j in range(chunks + 2):
         if j < chunks:
@@ -238,19 +264,22 @@
         size = units[u][2] // 4
         return pl.ds(pl.multiple_of(index * size, size), size)
 
-    def multiply(u):
+    def multiply(u, h, last):
         kind, j, _, _ = units[u]
+        rows = slice(None) if last and h == 0 else slice(h * depth // 2, (h + 1) * depth // 2)
         if kind == "own":
-            part[u][...] = dot(own[...], own[:, 2 * j * LANES:2 * (j + 1) * LANES])
+            product = dot(own[rows, :], own[rows, 2 * j * LANES:2 * (j + 1) * LANES])
         elif kind == "both":
-            part[u][...] = dot(own[...], jnp.concatenate([near[:, cols(j)], far[:, cols(j)]], 1))
+            product = dot(own[rows, :], jnp.concatenate([near[rows, cols(j)], far[rows, cols(j)]], 1))
         elif kind == "down":
-            part[u][...] = dot(near[:, :LANES * (j + 1)], far[:, cols(j)])
+            product = dot(near[rows, :LANES * (j + 1)], far[rows, cols(j)])
         else:
-            part[u][...] = dot(near[:, cols(j)], far[:, :LANES * j])
-        for p in range(2):
-            half_out[u][p] = part[u][rows_of(u, 2 * p + 1 - core), :].astype(BF16)
-        half_copy(u).start()
+            product = dot(near[rows, cols(j)], far[rows, :LANES * j])
+        part[u][...] = part[u][...] + product if h else product
+        if last:
+            for p in range(2):
+                half_out[u][p] = part[u][rows_of(u, 2 * p + 1 - core), :].astype(BF16)
+            half_copy(u).start()
 
     def fold_mate(u):
         half_copy(u).wait_recv()
@@ -303,19 +332,30 @@
             fold_opposite(to_opposite.pop(0)[1])
 
     for g, group in enumerate(groups):
-        if g:
-            pass_on((g, PIECES - 1))
-            far_copy(g - 1).wait_recv()
-            near_copy(g - 1).wait_recv()
-        for i, u in enumerate(group):
-            multiply(u)
-            if to_mate:
+        parts = halves(g - 1)
+        if g == chunks:
+            while to_mate:
                 done = to_mate.pop(0)
                 fold_mate(done[1])
                 to_opposite.append(done)
-            to_mate.append((g, u))
-            pass_on((g, i + 2))
-            drain(g - 4)
+        for h in parts:
+            if g:
+                if h == 0:
+                    pass_on((g, PIECES - 1))
+                far_copy(g - 1, h).wait_recv()
+                near_copy(g - 1, h).wait_recv()
+            last = h == parts[-1]
+            for i, u in enumerate(group):
+                multiply(u, h, last)
+                if not last:
+                    continue
+                if to_mate:
+                    done = to_mate.pop(0)
+                    fold_mate(done[1])
+                    to_opposite.append(done)
+                to_mate.append((g, u))
+                pass_on((g, i + 2))
+                drain(g - 4)
         pass_on((g, PIECES))
     for done in to_mate:
         fold_mate(done[1])
@@ -339,13 +379,13 @@
         wide = jnp.broadcast_to(total, (8, width))
         for q in range(4):
             turned = wide if q == 0 else pltpu.roll(wide, width - q * quarter, 1)
-            share[i, q] = turned[:, :2 * LANES]
+            share[i, q] = turned[0:1, :2 * LANES]
             share_copy(i, q).start()
     row_total = jnp.sum(row_own[...].T, 0, keepdims=True)
     for i in range(2):
         for q in range(4):
             share_arrival(i, q).wait_recv()
-            row_total = row_total + share_in[i, q, 0:1, :]
+            row_total = row_total + share_in[i, q]
     pairs = (1 + jnp.minimum(v, BAND) + jnp.minimum(chain - 1 - v, BAND)).astype(F32)
     squares = row_total * (1.0 / (samples * samples))
     result = squares / width + (squares / width - pairs) / (samples - 2)
@@ -355,17 +395,15 @@
         for k in (1, 2, 3):
             stat_copy(j, k).wait_send()
         each_send(j, lambda copy: copy.wait_send())
+        each_direct(j, lambda copy: copy.wait_send())
 
     @pl.when(last_in_ring)
     def _():
         for j, p in hops:
             near_relay(j, p).wait_send()
 
-    @pl.when(lands)
-    def _():
-        for j, p in hops:
-            if p < 2:
-                far_relay(j, p).wait_send()
+    for j in range(chunks):
+        by_side(lambda p: far_relay(j, p).wait_send(), lambda p: None)
 
     for u in range(count):
         half_copy(u).wait_send()
@@ -394,8 +432,8 @@
         pltpu.VMEM((width, LANES), F32),
         pltpu.VMEM((8, width), F32),
         pltpu.VMEM((8, width), F32),
-        pltpu.VMEM((2, 4, 8, 2 * LANES), F32),
-        pltpu.VMEM((2, 4, 8, 2 * LANES), F32),
+        pltpu.VMEM((2, 4, 1, 2 * LANES), F32),
+        pltpu.VMEM((2, 4, 1, 2 * LANES), F32),
     ]
     scratch += [pltpu.VMEM((rows, columns), F32) for _, _, rows, columns in units]
     for _ in range(2):
@@ -404,7 +442,7 @@
         scratch += [pltpu.VMEM((rows // 4, columns), BF16) for _, _, rows, columns in units]
     scratch += [
         dma((2, chunks)), dma((3, chunks)), dma((3, chunks)),
-        dma((chunks,)), dma((chunks,)), dma((chunks,)), dma((chunks,)),
+        dma((chunks + 1,)), dma((chunks + 1,)), dma((chunks + 1,)), dma((chunks + 1,)),
         dma((chunks, PIECES)), dma((chunks, PIECES)), dma((chunks, PIECES)), dma((chunks, PIECES)),
         dma((count,)), dma((count,)), dma((count,)), dma((count,)),
         dma((2, 4)), dma((2, 4)),

time: 126 us -> 120 us (0.952)
  Pallas kernels: 125 us -> 119 us
    pallas_call x1, Pallas kernels: 125 us -> 119 us  [local(): pl.pallas_call(functools.partial(kernel, chain, units), out_shape=jax.Sha...]
where the time goes in v3:
time: 120 us
  Pallas kernels  119 us (99%)
  local copies, waits for them, and re-layouts  1.24 us (1%)
    pallas_call x1, Pallas kernels, local(): pl.pallas_call(functools.partial(kernel, chain, units), out_shape=jax.Sha...  119 us

profile of v3, /device:TPU:1, one launch (start us, length us, event | category | flops | bytes accessed | tf_op | source)
XLA Modules:
  0.0 120.3 jit_solution(13959524668428308292)
XLA Ops:
  0.0 119.0 %shard_map.28 = f32[1,192]{1,0:T(1,128)} custom-call(bf16[2048,768]{1,0:T(8,128)(2,1)} %dose_hbm.1, s32[2048,768]{1,0:T(8,128)} %seen_hbm.1), custom_call_target="tpu_custom_call" | custom-call | tf_op jit(solution)/shard_map/pallas_call | solution.py:450
  119.0 1.2 %copy.4 = f32[192]{0:T(256)} copy(f32[192]{0:T(256)} %bitcast.1) | data formatting | bytes 1536
